TPU v7x, 512 devices: a whole 4x8x8 slice. The times are simulated.
512 devices in a mesh: ctx: 32 (over y, x), tp: 16 (over z, core).
Axes of the slice: x: 4, y: 8, z: 8, core: 2. Of those that a mesh axis runs over, the one named last changes fastest.
Arguments:
- query_states: bfloat16 [8192, 8192], P('ctx', 'tp'), may hold values from -250 to 250
- key_matrix: bfloat16 [8192, 1024], P('ctx'), may hold values from -8 to 8
- value_matrix: bfloat16 [8192, 1024], P('ctx'), may hold values from -6 to 6
- hidden: bfloat16 [8192, 14336], P('ctx', 'tp'), may hold values from -6 to 6
- down_weight: bfloat16 [14336, 8192], P('tp', 'ctx'), may hold values from -0.046875 to 0.046875
- out_weight: bfloat16 [8192, 8192], P('tp', 'ctx'), may hold values from -0.0625 to 0.0625
- encoder: bfloat16 [8192, 1024], P('ctx'), may hold values from -0.0625 to 0.0625
- decoder: bfloat16 [1024, 8192], P(None, 'tp'), may hold values from -0.1875 to 0.1875
- cotangent: bfloat16 [8192, 8192], P('ctx', 'tp'), may hold values from -6 to 6
Outputs:
- attended: bfloat16 [8192, 8192], P('ctx', 'tp')
- decoded: bfloat16 [8192, 8192], P('ctx', 'tp')
- grad_hidden: bfloat16 [8192, 14336], P('ctx', 'tp')
- grad_attended: bfloat16 [8192, 8192], P('ctx', 'tp')
All inputs are finite; a program needn't handle non-finite values.
Results may differ from a plain program's by a relative error of at most 0.035.
Values may be sent and summed in bfloat16 or wider, within the bound.
A program may use at most 64 MiB of HBM per device.

v0:
```python
import math

import jax
import jax.numpy as jnp
from jax import lax
from jax.sharding import PartitionSpec as P

HEAD_WIDTH = 128
QUERY_PER_KEY = 8


def per_device(
    query_states,
    key_matrix,
    value_matrix,
    hidden,
    down_weight,
    out_weight,
    encoder,
    decoder,
    cotangent,
):
    rows_here = query_states.shape[0]
    head_size = HEAD_WIDTH
    heads_here = query_states.shape[1] // head_size
    scale = 1.0 / math.sqrt(head_size)
    tp_index = lax.axis_index("tp")
    ctx_index = lax.axis_index("ctx")
    group_head = tp_index * heads_here // QUERY_PER_KEY
    key_cols = lax.dynamic_slice_in_dim(key_matrix, group_head * head_size, head_size, 1)
    value_cols = lax.dynamic_slice_in_dim(value_matrix, group_head * head_size, head_size, 1)
    query_heads = jnp.transpose(query_states.reshape(rows_here, heads_here, head_size), (1, 0, 2))
    first = ctx_index * rows_here
    last = first + rows_here - 1
    query_pos = first + jnp.arange(rows_here, dtype=jnp.int32)

    def block_step(carry, block):
        key_block, value_block, block_start = block

        def compute(state):
            top, total, summed = state
            scores = (
                jnp.einsum(
                    "hqd,kd->hqk", query_heads, key_block, preferred_element_type=jnp.float32
                )
                * scale
            )
            key_pos = block_start + jnp.arange(key_block.shape[0], dtype=jnp.int32)
            visible = key_pos[None, :] <= query_pos[:, None]
            scores = jnp.where(visible[None], scores, jnp.float32(-1e30))
            new_top = jnp.maximum(top, jnp.max(scores, axis=-1))
            factor = jnp.exp(top - new_top)
            weights = jnp.where(
                visible[None], jnp.exp(scores - new_top[..., None]), jnp.float32(0.0)
            )
            total = total * factor + jnp.sum(weights, axis=-1)
            update = jnp.einsum(
                "hqk,kd->hqd",
                weights.astype(jnp.bfloat16),
                value_block,
                preferred_element_type=jnp.float32,
            )
            summed = summed * factor[..., None] + update
            return (new_top, total, summed)

        live = (block_start >= 0) & (block_start <= last)
        return (lax.cond(live, compute, lambda state: state, carry), None)

    initial = (
        jnp.full((heads_here, rows_here), -1e30, jnp.float32),
        jnp.zeros((heads_here, rows_here), jnp.float32),
        jnp.zeros((heads_here, rows_here, head_size), jnp.float32),
    )
    carry = initial
    key_piece = lax.all_gather(key_cols, "ctx", axis=0, tiled=True)
    value_piece = lax.all_gather(value_cols, "ctx", axis=0, tiled=True)
    count = key_piece.shape[0]
    width = 512
    number = count // width
    key_blocks = key_piece.reshape(number, width, head_size)
    value_blocks = value_piece.reshape(number, width, head_size)
    starts = jnp.arange(number, dtype=jnp.int32) * width
    carry, unused = lax.scan(block_step, carry, (key_blocks, value_blocks, starts))
    state = carry
    top, total, summed = state
    result = summed / total[..., None]
    attended = (
        jnp.transpose(result, (1, 0, 2))
        .reshape(rows_here, heads_here * head_size)
        .astype(jnp.bfloat16)
    )
    grad_part = lax.dot_general(
        cotangent, decoder, (((1,), (1,)), ((), ())), preferred_element_type=jnp.float32
    )
    grad_code = lax.psum(grad_part.astype(jnp.bfloat16), "tp")
    stacked_weight = jnp.concatenate([down_weight, out_weight], axis=0)
    inputs = jnp.concatenate([hidden, attended], axis=1)
    hidden_here = hidden.shape[1]
    merged_share = lax.psum_scatter(
        jnp.dot(stacked_weight, encoder, preferred_element_type=jnp.float32).astype(jnp.bfloat16),
        "ctx",
        scatter_dimension=0,
        tiled=True,
    )
    piece = lax.all_gather(merged_share, "ctx", axis=0, tiled=True)
    code_part = jnp.dot(inputs, piece, preferred_element_type=jnp.float32)
    grad_cols = lax.dot_general(
        grad_code, piece, (((1,), (1,)), ((), ())), preferred_element_type=jnp.float32
    )
    grad_cols_all = grad_cols
    code_part, grad_cols_all = (code_part, grad_cols_all)
    code = lax.psum(code_part.astype(jnp.bfloat16), "tp")
    decoded = jnp.dot(code, decoder, preferred_element_type=jnp.float32).astype(jnp.bfloat16)
    grad_hidden = grad_cols_all[:, :hidden_here].astype(jnp.bfloat16)
    grad_attended = grad_cols_all[:, hidden_here:].astype(jnp.bfloat16)
    return (attended, decoded, grad_hidden, grad_attended)


def solution(mesh):
    return jax.shard_map(
        per_device,
        mesh=mesh,
        in_specs=(
            P("ctx", "tp"),
            P("ctx", None),
            P("ctx", None),
            P("ctx", "tp"),
            P("tp", "ctx"),
            P("tp", "ctx"),
            P("ctx", None),
            P(None, "tp"),
            P("ctx", "tp"),
        ),
        out_specs=(P("ctx", "tp"), P("ctx", "tp"), P("ctx", "tp"), P("ctx", "tp")),
        check_vma=False,
    )
```

profile of v0, /device:TPU:1, one launch (start us, length us, event | category | flops | bytes accessed | tf_op | source)
XLA Modules:
  0.0 425.6 jit_solution(3444915046034424703)
XLA Ops:
  7.2 1.6 constant_dynamic-slice_fusion.1
  8.9 1.5 constant_dynamic-slice_fusion
  10.4 3.8 convolution_convert_fusion
  14.2 84.1 %fusion.2 = bf16[48,1024]{1,0:T(8,128)(2,1)S(1)} fusion(bf16[1408,1024]{1,0:T(8,128)(2,1)} %convolution_convert_fusion), kind=kCustom, calls=%all-reduce-scatter | all-reduce-scatter fusion | flops 1572865 | bytes 2983936
  98.2 1.3 collective-permute-start
  99.6 1.3 collective-permute-start.1
  100.9 2.2 collective-permute-start.2
  103.1 1.3 dynamic-slice.4
  105.1 0.6 concatenate.8
  105.7 0.7 dynamic-slice_bitcast_fusion
  106.8 1.3 convolution_convert_fusion.2
  108.1 74.5 %all-gather.7.cloned.1.call-done = bf16[8192,128]{1,0:T(8,128)(2,1)} async-done(((bf16[256,128]{1,0:T(8,128)(2,1)}), bf16[8192,128]{1,0:T(8,128)(2,1)}) %all-gather.7.cloned.1.call-update) | async-done | bytes 2097168 | tf_op jit(solution)/shard_map/all_gather | solution.py:76
  182.6 35.4 %while.15 = (s32[]{:T(128)}, f32[4,256]{1,0:T(4,128)S(1)}, f32[4,256]{1,0:T(4,128)S(1)}, f32[4,256,128]{2,1,0:T(8,128)S(1)}, s32[16]{0:T(128)S(1)}, /*index=5*/s...) while((s32[]{:T(128)}, f32[4,256]{1,0:T(4,128)S(1)}, ...), condition=%wide.region_5.6_spmd.clone, body=%wide.region_0.5_spmd.clone.sunk | while | flops 275647232 | bytes 8463659 | solution.py:83
  182.6 0.6 dynamic_slice.43
  184.5 4.6 %conditional.3 = ((f32[4,256]{1,0:T(4,128)S(1)}, f32[4,256]{1,0:T(4,128)S(1)}, f32[4,256,128]{2,1,0:T(8,128)S(1)})) conditional(s32[]{:T(128)} %convert_element_type.50, (f32[4,256]{1,0:T(4,128)S(1)}, f32[4,256]{1,0:T(4,128)S(1)}, f32[4,256,128]{2,1,0:T(8,128)S(1)}) %tuple.44, (s32[]{:T(128)}, s32[]{:T(128)}, bf16[16,512,128]{2,1,0:T(8,128)(2,1)}, ...), branch_computations={%region_1.1_spmd, %region_2.4_spmd} | conditional | flops 275647232 | bytes 8462376 | solution.py:67
  184.5 0.7 iota_add_fusion
  185.4 1.4 fusion.3
  187.3 1.8 convolution_add_fusion
  189.1 0.6 dynamic_slice.43
  191.0 0.6 dynamic_slice.43
  193.0 0.6 dynamic_slice.43
  194.9 0.6 dynamic_slice.43
  196.8 0.6 dynamic_slice.43
  198.7 0.6 dynamic_slice.43
  218.2 50.9 %all-gather.9.cloned.1.call-done = bf16[32,44,1024]{2,1,0:T(8,128)(2,1)} async-done(((bf16[1,44,1024]{2,1,0:T(8,128)(2,1)}), bf16[32,44,1024]{2,1,0:T(8,128)(2,1)}) %all-gather.9.cloned.1.call-update) | async-done | bytes 2883600 | tf_op jit(solution)/shard_map/all_gather | solution.py:105
  269.2 5.2 %reshape.57 = bf16[1408,1024]{1,0:T(8,128)(2,1)} reshape(bf16[32,44,1024]{2,1,0:T(8,128)(2,1)} %all-gather.9.cloned.1.call-done) | data formatting | bytes 5767168
  274.4 3.6 convolution_convert_fusion.3
  278.0 135.4 %all-reduce.5.cloned.1.call-done = (bf16[256,1024]{1,0:T(8,128)(2,1)}, bf16[256,1024]{1,0:T(8,128)(2,1)}) async-done(((bf16[256,1024]{1,0:T(8,128)(2,1)}, bf16[256,1024]{1,0:T(8,128)(2,1)}), (bf16[256,1024]{1,0:T(8,128)(2,1)}, bf16[256,1024]{1,0:T(8,128)(2,1)})) %all-reduce.5.cloned.1.call-update) | async-done | bytes 1048592 | tf_op jit(solution)/shard_map/psum | solution.py:112
  413.4 3.0 convolution_convert_fusion.1
  416.4 0.8 slice.10
  417.3 0.7 slice.11
  418.0 1.1 convolution_convert_fusion.4
  (78 shorter events, 7.0 us)
Async XLA Ops:
  7.2 99.6 %copy-start = (bf16[1024,512]{1,0:T(8,128)(2,1)S(1)}, bf16[1024,512]{1,0:T(8,128)(2,1)}, u32[]{:S(2)}) copy-start(bf16[1024,512]{1,0:T(8,128)(2,1)} %param.20) | copy-start | bytes 3145732
  7.2 100.9 %all-gather.5.cloned.1.call-start = ((), (), s32[]{:S(2)}) async-start(), calls=%async_computation | async-start | bytes 2162688 | tf_op jit(solution)/shard_map/all_gather | solution.py:75
  8.8 173.7 %all-gather.7.cloned.1.call-start = ((), (), s32[]{:S(2)}) async-start(), calls=%async_computation.1 | async-start | bytes 2162688 | tf_op jit(solution)/shard_map/all_gather | solution.py:76
  10.4 258.8 %all-gather.9.cloned.1.call-start = ((), (), s32[]{:S(2)}) async-start(), calls=%async_computation.2 | async-start | bytes 3244032 | tf_op jit(solution)/shard_map/all_gather | solution.py:105
  14.2 92.3 %copy-start.4 = (bf16[256,512]{1,0:T(8,128)(2,1)S(1)}, bf16[256,512]{1,0:T(8,128)(2,1)}, u32[]{:S(2)}) copy-start(bf16[256,512]{1,0:T(8,128)(2,1)} %param.13) | copy-start | bytes 786436
  14.2 92.6 %copy-start.2 = (bf16[256,512]{1,0:T(8,128)(2,1)S(1)}, bf16[256,512]{1,0:T(8,128)(2,1)}, u32[]{:S(2)}) copy-start(bf16[256,512]{1,0:T(8,128)(2,1)} %param.21) | copy-start | bytes 786436
  98.2 6.8 %collective-permute-start = (bf16[48,1024]{1,0:T(8,128)(2,1)S(1)}, bf16[48,1024]{1,0:T(8,128)(2,1)S(1)}, u32[]{:S(2)}, u32[]{:S(2)}) collective-permute-start(bf16[48,1024]{1,0:T(8,128)(2,1)S(1)} %fusion.2), channel_id=1, source_target_pairs={{0,16},{16,32},{32,48},{48,64},{64,80},{80,96},{96,112},{112,128},... | collective-permute-start | bytes 294920
  99.6 5.5 %collective-permute-start.1 = (bf16[48,1024]{1,0:T(8,128)(2,1)S(1)}, bf16[48,1024]{1,0:T(8,128)(2,1)S(1)}, u32[]{:S(2)}, u32[]{:S(2)}) collective-permute-start(bf16[48,1024]{1,0:T(8,128)(2,1)S(1)} %fusion.2), channel_id=1, source_target_pairs={{0,32},{16,48},{32,64},{48,80},{64,96},{80,112},{96,128},{112,144}... | collective-permute-start | bytes 294920
  100.9 4.2 collective-permute-start.2
  106.4 307.0 %all-reduce.5.cloned.1.call-start = ((), (), s32[]{:S(2)}) async-start(), calls=%async_computation.3 | async-start | bytes 2097152 | tf_op jit(solution)/shard_map/psum | solution.py:112
  218.2 56.2 %copy-start.3 = (bf16[256,512]{1,0:T(8,128)(2,1)}, bf16[256,512]{1,0:T(8,128)(2,1)S(1)}, u32[]{:S(2)}) copy-start(bf16[256,512]{1,0:T(8,128)(2,1)S(1)} %copy_bitcast_fusion) | copy-start | bytes 786436
  218.2 56.2 %copy-start.5 = (bf16[256,896]{1,0:T(8,128)(2,1)S(1)}, bf16[256,896]{1,0:T(8,128)(2,1)}, u32[]{:S(2)}) copy-start(bf16[256,896]{1,0:T(8,128)(2,1)} %param.16) | copy-start | bytes 1376260
  413.4 4.6 %copy-start.1 = (bf16[256,1024]{1,0:T(8,128)(2,1)S(1)}, bf16[256,1024]{1,0:T(8,128)(2,1)}, u32[]{:S(2)}) copy-start(bf16[256,1024]{1,0:T(8,128)(2,1)} %get-tuple-element.211) | copy-start | bytes 1572868
Sparse Core Ops, SparseCore 0:
  11.8 86.9 all-gather.4
  102.4 80.0 all-gather.6
  186.3 82.8 all-gather.8
  278.1 135.2 all-reduce.4
where the time goes:
time: 427 us; the launch traced here: 426 us
  waiting for transfers between devices  261 us (61%)
  blocking collectives  84.1 us (20%)
  local copies, waits for them, and re-layouts  22.2 us (5%)
  loops' own time  21.5 us (5%)
  matrix products  15.9 us (4%)
  between operations  14.6 us (3%)
  starting transfers between devices  4.98 us (1%)
    psum x1, waiting for transfers between devices, per_device(): code = lax.psum(code_part.astype(jnp.bfloat16), 'tp')  135 us
    unnamed x1, blocking collectives  84.1 us
    all_gather x1, waiting for transfers between devices, per_device(): value_piece = lax.all_gather(value_cols, 'ctx', axis=0, tiled=True)  74.5 us
    all_gather x1, waiting for transfers between devices, per_device(): piece = lax.all_gather(merged_share, 'ctx', axis=0, tiled=True)  50.9 us
    another operation x1, loops' own time, per_device(): lax.scan(block_step, carry, (key_blocks, value_blocks, starts))  21.2 us
    dynamic_slice x16, local copies, waits for them, and re-layouts, per_device(): lax.scan(block_step, carry, (key_blocks, value_blocks, starts))  9.39 us
  transfers between devices with their start and end apart: 7, of which 3 were waited for; matrix products, arithmetic and copies ran while one was open for 25% of the time, Pallas kernels for 0%

commit v1 on v0

v1 whole, which is shorter than its diff:
```python
import functools
import math

import jax
import jax.numpy as jnp
from jax import lax
from jax.experimental import pallas as pl
from jax.experimental.pallas import tpu as pltpu
from jax.sharding import PartitionSpec as P

MESH = pl.DeviceIdType.MESH
F32, BF16 = jnp.float32, jnp.bfloat16
NX, NY, NT = 4, 8, 16
ROWS = 256
HEAD = 128
HEADS = 4
R = 1024
LANES = 128
BLOCKS = R // LANES
FF_HERE, ATT_HERE = 896, 512
SLICE = ROWS // NT
GROUPS = 2
GROUP_COLS = R // GROUPS
EXP_SCALE = math.log2(math.e) / math.sqrt(HEAD)
PARTS = (("a", 0, 640, "x"), ("b", 640, 512, "x"), ("c", 1152, 256, "y"))
RING = {"x": NX, "y": NY}


def nt_dot(a, b):
    return lax.dot_general(a, b, (((1,), (1,)), ((), ())), preferred_element_type=F32)


def dot(a, b):
    return jnp.dot(a, b, preferred_element_type=F32)


def hops(n, way, half):
    return n // 2 if way == half else n // 2 - 1


def ring_order(n):
    steps = []
    for j in range(n // 2):
        step = []
        for way in (0, 1):
            for half in (way, 1 - way):
                k = hops(n, way, half) - j
                if k >= 1:
                    step.append((way, half, k))
        steps.append(step)
    return steps


def copies_of_ring(n):
    return 2 * (n - 1)


SEMS = sum(2 * (copies_of_ring(NX) + copies_of_ring(NY)) for _ in PARTS)
SEMS += (copies_of_ring(NX) + copies_of_ring(NY)) + 2 * NY
LOCAL = 16


def scratch_of(part):
    name, base, rows, first = part
    r = rows // NX
    second = "y" if first == "x" else "x"
    n1, n2 = RING[first], RING[second]
    return [
        pltpu.VMEM((2, n1 - 1, n2 // 2, r, LANES), BF16),
        pltpu.VMEM((2, n1 - 1, n2 // 2, r, LANES), BF16),
        pltpu.VMEM((n2, r, LANES), F32),
        pltpu.VMEM((2, n2 - 1, 1, r // 2, LANES), BF16),
        pltpu.VMEM((2, n2 - 1, 1, r // 2, LANES), BF16),
        pltpu.VMEM((NY, NX, r, LANES), BF16),
    ]


def kernel(*refs):
    q_in, k_in, v_in, hid_in, dw_in, ow_in, enc_in, dec_in, cot_in = refs[:9]
    att_out, dec_out, gh_out, ga_out = refs[9:13]
    rest = list(refs[13:])

    def take(count):
        taken = rest[:count]
        del rest[:count]
        return taken

    qv, hid, wv, enc, dec, cot, kv = take(7)
    acc, top, att, decd, gh, ga = take(6)
    gpart, grecv, gfull = take(3)
    cpart, crecv, cfull = take(3)
    bufs = {part[0]: take(6) for part in PARTS}
    send_sem, recv_sem, z_send, z_recv, local_sem = take(5)
    assert not rest

    ctx = lax.axis_index("ctx")
    tp = lax.axis_index("tp")
    y, x = lax.div(ctx, NX), lax.rem(ctx, NX)
    zi, core = lax.div(tp, 2), lax.rem(tp, 2)
    sibling = zi * 2 + 1 - core
    pos = {"x": x, "y": y}

    def shifted(axis, by):
        n = RING[axis]
        return lax.rem(pos[axis] + by + 2 * n, n)

    def neighbour(axis, by):
        if axis == "x":
            return {"ctx": y * NX + shifted("x", by)}
        return {"ctx": shifted("y", by) * NX + x}

    loads = {}

    def load(name, src, dst):
        copy = pltpu.make_async_copy(src, dst, local_sem.at[len(loads)])
        copy.start()
        loads[name] = copy

    head_cols = pl.ds(pl.multiple_of(zi * HEAD, HEAD), HEAD)
    half_rows = pl.ds(pl.multiple_of(core * 128, 128), 128)
    load("k", k_in.at[half_rows, head_cols], kv.at[0, core, y, x])
    load("v", v_in.at[half_rows, head_cols], kv.at[1, core, y, x])
    load("dw", dw_in, wv.at[pl.ds(0, FF_HERE)])
    load("ow", ow_in, wv.at[pl.ds(FF_HERE, ATT_HERE)])
    load("enc", enc_in, enc)
    load("cot", cot_in, cot)
    load("dec", dec_in, dec)
    load("q", q_in, qv)
    load("hid", hid_in, hid)

    barrier = pltpu.get_barrier_semaphore()
    for axis in ("x", "y"):
        for by in (1, -1):
            pl.semaphore_signal(barrier, inc=1, device_id=neighbour(axis, by), device_id_type=MESH)

    def greet(o, carry):
        pl.semaphore_signal(barrier, inc=1, device_id={"tp": lax.rem(tp + o, NT)}, device_id_type=MESH)
        return carry

    lax.fori_loop(1, NT, greet, 0)
    pl.semaphore_wait(barrier, 4 + NT - 1)

    started = []
    used = [0]

    def remote(src, dst, device, sem):
        return pltpu.make_async_remote_copy(
            src_ref=src,
            dst_ref=dst,
            send_sem=send_sem.at[sem],
            recv_sem=recv_sem.at[sem],
            device_id=device,
            device_id_type=MESH,
        )

    def send(src, dst, device, sem):
        copy = remote(src, dst, device, sem)
        copy.start()
        started.append(copy)

    def sems(count):
        first = used[0]
        used[0] += count
        return first

    def all_gather(axis, region):
        n = RING[axis]
        order = ring_order(n)
        number = {}
        for step in order:
            for item in step:
                number[item] = len(number)
        first = sems(len(number))
        for j, step in enumerate(order):
            for way, half, k in step:
                by = 1 if way == 0 else -1
                here = hops(n, way, half) - k
                if here > 0:
                    place = region(shifted(axis, -by * here), half)
                    remote(place, place, neighbour(axis, by), first + number[(way, half, k + 1)]).wait_recv()
                place = region(shifted(axis, -by * here), half)
                send(place, place, neighbour(axis, by), first + number[(way, half, k)])
            if j:
                yield j
            else:
                yield 0
            if j + 1 < len(order):
                for way, half, k in step:
                    if k == 1:
                        by = 1 if way == 0 else -1
                        place = region(shifted(axis, -by * (hops(n, way, half))), half)
                        remote(place, place, neighbour(axis, by), first + number[(way, half, 1)]).wait_recv()
        for way, half, k in order[-1]:
            by = 1 if way == 0 else -1
            place = region(shifted(axis, -by * hops(n, way, half)), half)
            remote(place, place, neighbour(axis, by), first + number[(way, half, 1)]).wait_recv()

    def reduce_scatter(axis, own_term, sbuf, rbuf, finish):
        n = RING[axis]
        order = ring_order(n)
        number, slot = {}, {}
        for step in order:
            for item in step:
                number[item] = len(number)
        for way in (0, 1):
            for i, item in enumerate([m for step in order for m in step if m[0] == way]):
                slot[item] = i
        first = sems(len(number))

        def arrival(item):
            way = item[0]
            place = rbuf.at[way, slot[item]]
            remote(sbuf.at[way, slot[item]], place, neighbour(axis, 1 if way == 0 else -1), first + number[item]).wait_recv()

        for j, step in enumerate(order):
            for item in step:
                way, half, k = item
                by = 1 if way == 0 else -1
                pieces = own_term(shifted(axis, by * k), half)
                before = (way, half, k + 1)
                if before in number:
                    arrival(before)
                    pieces = [p + rbuf[way, slot[before], i].astype(F32) for i, p in enumerate(pieces)]
                for i, p in enumerate(pieces):
                    sbuf[way, slot[item], i] = p.astype(BF16)
                send(sbuf.at[way, slot[item]], rbuf.at[way, slot[item]], neighbour(axis, by), first + number[item])
            yield j
        for half in (0, 1):
            pieces = own_term(pos[axis], half)
            for way in (0, 1):
                arrival((way, half, 1))
                pieces = [p + rbuf[way, slot[(way, half, 1)], i].astype(F32) for i, p in enumerate(pieces)]
            finish(half, pieces)

    def merged(part):
        name, base, rows, axis = part
        r = rows // NX
        sbuf1, rbuf1, share, sbuf2, rbuf2, whole = bufs[name]
        other = "y" if axis == "x" else "x"
        n2 = RING[other]

        def term_x(dest, half):
            start = pl.multiple_of(base + dest * r, 16)
            out = dot(wv[pl.ds(start, r), :], enc[:, half * (R // 2) : (half + 1) * (R // 2)])
            return [out[:, i * LANES : (i + 1) * LANES] for i in range(NY // 2)]

        def term_y(dest, half):
            count = rows // 2
            cols = pl.ds(pl.multiple_of(dest * LANES, LANES), LANES)
            out = dot(wv[pl.ds(base + half * count, count), :], enc[:, cols])
            return [out[i * r : (i + 1) * r] for i in range(NX // 2)]

        def keep(half, pieces):
            for i, p in enumerate(pieces):
                share[half * (n2 // 2) + i] = p

        def term_share(dest, half):
            return [share[dest, half * (r // 2) : (half + 1) * (r // 2)]]

        def keep_sum(half, pieces):
            whole[y, x, half * (r // 2) : (half + 1) * (r // 2)] = pieces[0].astype(BF16)

        yield from reduce_scatter(axis, term_x if axis == "x" else term_y, sbuf1, rbuf1, keep)
        yield from reduce_scatter(other, term_share, sbuf2, rbuf2, keep_sum)

        def rows_of(half):
            return pl.ds(half * (r // 2), r // 2)

        if axis == "x":
            yield from all_gather("y", lambda i, half: whole.at[i, x, rows_of(half)])
            yield from all_gather("x", lambda i, half: whole.at[pl.ds(half * (NY // 2), NY // 2), i])
        else:
            yield from all_gather("x", lambda i, half: whole.at[y, i, rows_of(half)])
            yield from all_gather("y", lambda i, half: whole.at[i, pl.ds(half * (NX // 2), NX // 2)])
        yield "done"

    def attend(row, diagonal):
        def one_head(h, carry):
            lanes = pl.ds(pl.multiple_of(h * HEAD, HEAD), HEAD)
            keys = kv[0, :, row].reshape(NX * ROWS, HEAD)
            values = kv[1, :, row].reshape(NX * ROWS, HEAD)
            s = nt_dot(qv[:, lanes], keys)
            if diagonal:
                at = lax.broadcasted_iota(jnp.int32, s.shape, 1)
                place = (lax.shift_right_logical(at, 7) & 3) * ROWS + lax.shift_right_logical(at, 9) * 128 + (at & 127)
                mine = x * ROWS + lax.broadcasted_iota(jnp.int32, s.shape, 0)
                s = jnp.where(place <= mine, s, F32(-1e30))
            new_top = jnp.max(s, axis=1, keepdims=True)
            if not diagonal:
                old_top = top[h][:, :1]
                new_top = jnp.maximum(old_top, new_top)
            weights = jnp.exp2((s - new_top) * F32(EXP_SCALE)).astype(BF16)
            extended = jnp.concatenate([values, jnp.ones_like(values)], axis=1)
            update = dot(weights, extended)
            if not diagonal:
                update = update + acc[h] * jnp.exp2((old_top - new_top) * F32(EXP_SCALE))
            acc[h] = update
            top[h] = jnp.broadcast_to(new_top, (ROWS, LANES))
            return carry

        lax.fori_loop(0, HEADS, one_head, 0)

    def keys_and_values():
        yield from all_gather("x", lambda i, half: kv.at[half, core, y, i])
        gather = all_gather("y", lambda i, half: kv.at[half, core, i])

        def hand_over(row):
            first = sems(2)
            for half in (0, 1):
                place = kv.at[half, core, row]
                send(place, place, {"tp": sibling}, first + half)
            return first

        def handed(row, first):
            for half in (0, 1):
                place = kv.at[half, 1 - core, row]
                remote(place, place, {"tp": sibling}, first + half).wait_recv()

        next(gather)
        first = hand_over(y)
        yield "sent"
        handed(y, first)
        attend(y, True)
        yield "attended"
        for k in range(1, NY // 2 + 1):
            if k < NY // 2:
                next(gather)
            else:
                for _ in gather:
                    pass
            rows = [shifted("y", -k), shifted("y", k)] if k < NY // 2 else [shifted("y", k)]
            firsts = [hand_over(row) for row in rows]
            yield "sent"
            for row, first in zip(rows, firsts):
                handed(row, first)

                @pl.when(row < y)
                def _():
                    attend(row, False)

                yield "attended"
        yield "done"

    def exchange(part_ref, recv_ref, full_ref, sem):
        def give(o, carry):
            to = lax.rem(tp + o, NT)
            pltpu.make_async_remote_copy(
                src_ref=part_ref.at[pl.ds(pl.multiple_of(to * SLICE, SLICE), SLICE)],
                dst_ref=recv_ref.at[o - 1],
                send_sem=z_send.at[sem],
                recv_sem=z_recv.at[sem],
                device_id={"tp": to},
                device_id_type=MESH,
            ).start()
            return carry

        lax.fori_loop(1, NT, give, 0)
        yield "given"
        mine = pl.ds(pl.multiple_of(tp * SLICE, SLICE), SLICE)
        pltpu.make_async_copy(recv_ref, recv_ref, z_recv.at[sem]).wait()
        total = part_ref[mine].astype(F32)
        for o in range(NT - 1):
            total = total + recv_ref[o].astype(F32)
        full_ref[mine] = total.astype(BF16)

        def share(o, carry):
            to = lax.rem(tp + o, NT)
            pltpu.make_async_remote_copy(
                src_ref=full_ref.at[mine],
                dst_ref=full_ref.at[mine],
                send_sem=z_send.at[sem + 1],
                recv_sem=z_recv.at[sem + 1],
                device_id={"tp": to},
                device_id_type=MESH,
            ).start()
            return carry

        lax.fori_loop(1, NT, share, 0)
        yield "shared"
        pltpu.make_async_copy(recv_ref, recv_ref, z_recv.at[sem + 1]).wait()
        yield "done"
        for i in (0, 1):
            pltpu.make_async_copy(recv_ref, recv_ref, z_send.at[sem + i]).wait()

    def step(gen, count=1):
        for _ in range(count):
            next(gen, None)

    def finish(gen):
        for _ in gen:
            pass

    kvs = keys_and_values()
    a, b, c = (merged(part) for part in PARTS)

    loads["k"].wait()
    loads["v"].wait()
    step(kvs)
    loads["dw"].wait()
    loads["ow"].wait()
    loads["enc"].wait()
    step(a)
    step(c)
    step(kvs)
    loads["cot"].wait()
    loads["dec"].wait()
    gpart[...] = nt_dot(cot[...], dec[...]).astype(BF16)
    grad = exchange(gpart, grecv, gfull, 0)
    step(grad)
    step(kvs)
    step(c)
    step(a)
    step(b)
    step(c)
    loads["q"].wait()
    step(kvs)
    step(c)
    step(kvs)
    step(c)
    step(a)
    step(grad)
    step(kvs)
    step(a)
    step(c)
    step(kvs)
    step(a)
    step(b)
    step(c)
    step(a)
    step(kvs)
    step(c)
    step(a)
    step(kvs)
    step(a)
    step(c)
    step(kvs)
    step(a)
    step(b)
    step(c)
    step(a)
    step(b)
    step(kvs)
    step(a)
    step(b)
    step(c)
    step(kvs)
    step(b)
    step(c)
    step(kvs)
    step(b)
    step(kvs)
    step(b)
    step(a)
    step(b)
    step(kvs)
    step(b)
    finish(kvs)

    def divide(h, carry):
        lanes = pl.ds(pl.multiple_of(h * HEAD, HEAD), HEAD)
        state = acc[h]
        att[:, lanes] = (state[:, :HEAD] / state[:, HEAD:]).astype(BF16)
        return carry

    lax.fori_loop(0, HEADS, divide, 0)
    outs = []

    def store(src, dst):
        copy = pltpu.make_async_copy(src, dst, local_sem.at[len(loads) + len(outs)])
        copy.start()
        outs.append(copy)

    store(att, att_out)
    step(b)
    finish(a)
    finish(c)
    finish(grad)
    step(b)
    finish(b)
    whole = {name: bufs[name][5] for name, *_ in PARTS}

    loads["hid"].wait()

    def columns(name, rows, j):
        lo = whole[name][2 * j].reshape(rows, LANES)
        hi = whole[name][2 * j + 1].reshape(rows, LANES)
        return jnp.concatenate([lo, hi], axis=1)

    codes = []
    for g in range(GROUPS):
        for j in range(BLOCKS // 2 // GROUPS):
            at = g * (BLOCKS // 2 // GROUPS) + j
            ma, mb, mc = columns("a", 640, at), columns("b", 512, at), columns("c", 256, at)
            total = dot(hid[:, :640], ma) + dot(hid[:, 640:], mb[:256])
            total = total + dot(att[:, :256], mb[256:]) + dot(att[:, 256:], mc)
            cpart[g, :, 256 * j : 256 * (j + 1)] = total.astype(BF16)
        gen = exchange(cpart.at[g], crecv.at[g], cfull.at[g], 2 + 2 * g)
        step(gen)
        codes.append(gen)

    def back(name, rows):
        total = None
        for j in range(BLOCKS // 2):
            term = nt_dot(gfull[:, 256 * j : 256 * (j + 1)], columns(name, rows, j))
            total = term if total is None else total + term
        return total.astype(BF16)

    gh[:, :640] = back("a", 640)
    step(codes[0])
    from_b = back("b", 512)
    gh[:, 640:] = from_b[:, :256]
    store(gh, gh_out)
    step(codes[1])
    ga[:, :256] = from_b[:, 256:]
    ga[:, 256:] = back("c", 256)
    store(ga, ga_out)
    for copy in started:
        copy.wait_send()
    step(codes[0])
    result = dot(cfull[0], dec[:GROUP_COLS])
    step(codes[1])
    decd[...] = (result + dot(cfull[1], dec[GROUP_COLS:])).astype(BF16)
    store(decd, dec_out)
    for gen in codes:
        finish(gen)
    for copy in outs:
        copy.wait()


def per_device(*args):
    anywhere = pl.BlockSpec(memory_space=pl.ANY)
    scratch = [
        pltpu.VMEM((ROWS, ATT_HERE), BF16),
        pltpu.VMEM((ROWS, FF_HERE), BF16),
        pltpu.VMEM((FF_HERE + ATT_HERE, 256), BF16),
        pltpu.VMEM((256, R), BF16),
        pltpu.VMEM((R, 512), BF16),
        pltpu.VMEM((ROWS, 512), BF16),
        pltpu.VMEM((2, 2, NY, NX, 128, HEAD), BF16),
        pltpu.VMEM((HEADS, ROWS, 2 * HEAD), F32),
        pltpu.VMEM((HEADS, ROWS, LANES), F32),
        pltpu.VMEM((ROWS, ATT_HERE), BF16),
        pltpu.VMEM((ROWS, 512), BF16),
        pltpu.VMEM((ROWS, FF_HERE), BF16),
        pltpu.VMEM((ROWS, ATT_HERE), BF16),
        pltpu.VMEM((ROWS, R), BF16),
        pltpu.VMEM((NT - 1, SLICE, R), BF16),
        pltpu.VMEM((ROWS, R), BF16),
        pltpu.VMEM((GROUPS, ROWS, GROUP_COLS), BF16),
        pltpu.VMEM((GROUPS, NT - 1, SLICE, GROUP_COLS), BF16),
        pltpu.VMEM((GROUPS, ROWS, GROUP_COLS), BF16),
    ]
    for part in PARTS:
        scratch += scratch_of(part)
    scratch += [
        pltpu.SemaphoreType.DMA((SEMS,)),
        pltpu.SemaphoreType.DMA((SEMS,)),
        pltpu.SemaphoreType.DMA((2 + 2 * GROUPS,)),
        pltpu.SemaphoreType.DMA((2 + 2 * GROUPS,)),
        pltpu.SemaphoreType.DMA((LOCAL,)),
    ]
    return pl.pallas_call(
        kernel,
        out_shape=(
            jax.ShapeDtypeStruct((ROWS, ATT_HERE), BF16),
            jax.ShapeDtypeStruct((ROWS, 512), BF16),
            jax.ShapeDtypeStruct((ROWS, FF_HERE), BF16),
            jax.ShapeDtypeStruct((ROWS, ATT_HERE), BF16),
        ),
        in_specs=[anywhere] * 9,
        out_specs=(anywhere,) * 4,
        scratch_shapes=scratch,
        compiler_params=pltpu.CompilerParams(
            collective_id=0, has_side_effects=True, vmem_limit_bytes=56 * 1024 * 1024
        ),
    )(*args)


def solution(mesh):
    return jax.shard_map(
        per_device,
        mesh=mesh,
        in_specs=(
            P("ctx", "tp"),
            P("ctx", None),
            P("ctx", None),
            P("ctx", "tp"),
            P("tp", "ctx"),
            P("tp", "ctx"),
            P("ctx", None),
            P(None, "tp"),
            P("ctx", "tp"),
        ),
        out_specs=(P("ctx", "tp"), P("ctx", "tp"), P("ctx", "tp"), P("ctx", "tp")),
        check_vma=False,
    )
```

time: 427 us -> 141 us (0.33)
  waiting for transfers between devices: 261 us -> 0 us
  Pallas kernels: 0 us -> 136 us
  blocking collectives: 84.1 us -> 0 us
  loops' own time: 21.5 us -> 0 us
  local copies, waits for them, and re-layouts: 22.2 us -> 4.24 us
  matrix products: 15.9 us -> 0 us
  between operations: 14.6 us -> 0.66 us
  starting transfers between devices: 4.98 us -> 0 us
    pallas_call x0 -> x1, Pallas kernels: none -> 136 us  [per_device(): pl.pallas_call(kernel, out_shape=(jax.ShapeDtypeStruct((ROWS, ATT_HERE),...]
    psum x1 -> x0, waiting for transfers between devices: 135 us -> none  [per_device(): code = lax.psum(code_part.astype(jnp.bfloat16), 'tp')]
    all_gather x3 -> x0, waiting for transfers between devices: 125 us -> none  [the longest x1 74.5 us: per_device(): value_piece = lax.all_gather(value_cols, 'ctx', axis=0, tiled=True)]
    unnamed x1 -> x0, blocking collectives: 84.1 us -> none
    another operation x17 -> x0, loops' own time: 21.5 us -> none  [the longest x1 21.2 us: per_device(): lax.scan(block_step, carry, (key_blocks, value_blocks, starts))]
    dot_general x7 -> x0, matrix products: 15.9 us -> none  [the longest x1 3.76 us: per_device(): jnp.dot(stacked_weight, encoder, preferred_element_type=jnp.float32)]
    dynamic_slice x18 -> x0, local copies, waits for them, and re-layouts: 12.4 us -> none  [the longest x16 9.39 us: per_device(): lax.scan(block_step, carry, (key_blocks, value_blocks, starts))]
    unnamed x3 -> x0, starting transfers between devices: 4.82 us -> none
  transfers between devices with their start and end apart: 7 -> 0, of which waited for: 3 -> 0; matrix products, arithmetic and copies ran while one was open for 25% -> 0% of each run, Pallas kernels for 0% -> 0%
where the time goes in v1:
time: 141 us
  Pallas kernels  136 us (96%)
  local copies, waits for them, and re-layouts  4.24 us (3%)
    pallas_call x1, Pallas kernels, per_device(): pl.pallas_call(kernel, out_shape=(jax.ShapeDtypeStruct((ROWS, ATT_HERE),...  136 us
    unnamed x10, local copies, waits for them, and re-layouts  4.24 us

profile of v1, /device:TPU:1, one launch (start us, length us, event | category | flops | bytes accessed | tf_op | source)
XLA Modules:
  0.0 141.1 jit_solution(16816853603918783056)
XLA Ops:
  0.6 136.2 %shard_map.120 = (bf16[256,512]{1,0:T(8,128)(2,1)}, bf16[256,512]{1,0:T(8,128)(2,1)}, bf16[256,896]{1,0:T(8,128)(2,1)}, bf16[256,512]{1,0:T(8,128)(2,1)}) custom-call(bf16[256,512]{1,0:T(8,128)(2,1)} %refs_0_.1, bf16[256,1024]{1,0:T(8,128)(2,1)} %refs_1_.1, bf16[256,1024]{1,0:T(8,128)(2,1)} %refs_2_.1, bf16[256,896]{1,0:T(8,128)(2,1)} %refs_3_.1, ...), custom_call_target="tpu_custom_call" | custom-call | tf_op jit(solution)/shard_map/pallas_call | solution.py:562
  136.8 0.0 copy-start.2
  136.8 0.0 copy-start
  136.9 1.7 %copy.17 = bf16[256,512]{1,0:T(8,128)(2,1)} copy(bf16[256,512]{1,0:T(8,128)(2,1)} %get-tuple-element.8) | data formatting | bytes 524288
  138.6 0.0 copy-done.2
  138.6 0.7 copy.18
  139.3 0.0 copy-done
  139.3 0.0 copy-start.1
  139.3 0.8 copy.19
  140.1 0.3 copy-done.1
  140.4 0.7 copy.20
Async XLA Ops:
  136.8 1.8 %copy-start.2 = (bf16[256,512]{1,0:T(8,128)(2,1)S(1)}, bf16[256,512]{1,0:T(8,128)(2,1)}, u32[]{:S(2)}) copy-start(bf16[256,512]{1,0:T(8,128)(2,1)} %get-tuple-element.9) | copy-start | bytes 786436
  136.8 2.5 %copy-start = (bf16[256,896]{1,0:T(8,128)(2,1)S(1)}, bf16[256,896]{1,0:T(8,128)(2,1)}, u32[]{:S(2)}) copy-start(bf16[256,896]{1,0:T(8,128)(2,1)} %get-tuple-element.10) | copy-start | bytes 1376260
  139.3 1.1 copy-start.1

commit v2 on v1

v2 whole, which is shorter than its diff:
```python
import functools
import math

import jax
import jax.numpy as jnp
from jax import lax
from jax.experimental import pallas as pl
from jax.experimental.pallas import tpu as pltpu
from jax.sharding import PartitionSpec as P

MESH = pl.DeviceIdType.MESH
F32, BF16 = jnp.float32, jnp.bfloat16
NX, NY, NT = 4, 8, 16
ROWS = 256
HEAD = 128
HEADS = 4
R = 1024
LANES = 128
BLOCKS = R // LANES
FF_HERE, ATT_HERE = 896, 512
SLICE = ROWS // NT
ORDER = (
    "kagkcbabkgacukabcuaukgubkkuuubcaukuuubuuaukubuuuca",
    "kubuukauuuubcukua02cu013cbck31g20kau3ck12mbuucmccm",
    "bckcgckga3uu",
)
READY = (9, 10, 11, 12)
GROUPS = ((0, 1, -1), (2, -2), (3, -3), (4,))
EXP_SCALE = math.log2(math.e) / math.sqrt(HEAD)
PARTS = (("a", 0, 512, "y"), ("b", 512, 384, "y"), ("c", 896, 512, "x"))
SPLIT = PARTS[0][2]
RING = {"x": NX, "y": NY}


def nt_dot(a, b):
    return lax.dot_general(a, b, (((1,), (1,)), ((), ())), preferred_element_type=F32)


def dot(a, b):
    return jnp.dot(a, b, preferred_element_type=F32)


def hops(n, way, half):
    return n // 2 if way == half else n // 2 - 1


def ring_order(n):
    steps = []
    for j in range(n // 2):
        step = []
        for way in (0, 1):
            for half in (way, 1 - way):
                k = hops(n, way, half) - j
                if k >= 1:
                    step.append((way, half, k))
        steps.append(step)
    return steps


def copies_of_ring(n):
    return 2 * (n - 1)


SEMS = sum(2 * copies_of_ring(RING[part[3]]) + 2 for part in PARTS)
SEMS += copies_of_ring(NY) + NY * (copies_of_ring(NX) + 2)
LOCAL = 16


def scratch_of(part):
    name, base, rows, first = part
    r = rows // NX
    second = "y" if first == "x" else "x"
    n1, n2 = RING[first], RING[second]
    return [
        pltpu.VMEM((NY, NX, r, LANES), F32),
        pltpu.VMEM((2, n1 - 1, n2 // 2, r, LANES), BF16),
        pltpu.VMEM((2, n1 - 1, n2 // 2, r, LANES), BF16),
        pltpu.VMEM((n2, r, LANES), F32),
        pltpu.VMEM((n2, r, LANES), BF16),
        pltpu.VMEM((n2 - 1, r, LANES), BF16),
        pltpu.VMEM((NY, NX, r, LANES), BF16),
    ]


def kernel(*refs):
    q_in, k_in, v_in, hid_in, dw_in, ow_in, enc_in, dec_in, cot_in = refs[:9]
    att_out, dec_out, gh_out, ga_out = refs[9:13]
    rest = list(refs[13:])

    def take(count):
        taken = rest[:count]
        del rest[:count]
        return taken

    qv, hid, wv, enc, dec, cot, kv = take(7)
    acc, top, att, decd, gh, ga = take(6)
    grad_refs = take(5)
    code_refs = [take(5) for _ in GROUPS]
    bufs = {part[0]: take(7) for part in PARTS}
    send_sem, recv_sem, z_send, z_recv, local_sem = take(5)
    assert not rest

    ctx = lax.axis_index("ctx")
    tp = lax.axis_index("tp")
    y, x = lax.div(ctx, NX), lax.rem(ctx, NX)
    zi, core = lax.div(tp, 2), lax.rem(tp, 2)
    sibling = zi * 2 + 1 - core
    pos = {"x": x, "y": y}

    def shifted(axis, by):
        n = RING[axis]
        return lax.rem(pos[axis] + by + 2 * n, n)

    def neighbour(axis, by):
        if axis == "x":
            return {"ctx": y * NX + shifted("x", by)}
        return {"ctx": shifted("y", by) * NX + x}

    loads = {}

    def load(name, src, dst):
        copy = pltpu.make_async_copy(src, dst, local_sem.at[len(loads)])
        copy.start()
        loads[name] = copy

    head_cols = pl.ds(pl.multiple_of(zi * HEAD, HEAD), HEAD)
    half_rows = pl.ds(pl.multiple_of(core * 128, 128), 128)
    load("k", k_in.at[half_rows, head_cols], kv.at[0, core, y, x])
    load("v", v_in.at[half_rows, head_cols], kv.at[1, core, y, x])
    load("dw", dw_in, wv.at[pl.ds(0, FF_HERE)])
    load("ow", ow_in, wv.at[pl.ds(FF_HERE, ATT_HERE)])
    load("enc", enc_in, enc)
    load("cot", cot_in, cot)
    load("dec", dec_in, dec)
    load("q", q_in, qv)
    load("hid", hid_in, hid)

    barrier = pltpu.get_barrier_semaphore()

    def greet(device):
        pl.semaphore_signal(barrier, inc=1, device_id=device, device_id_type=MESH)

    for axis in ("x", "y"):
        for by in range(1, RING[axis]):
            greet(neighbour(axis, by))

    def greet_tp(o, carry):
        greet({"tp": lax.rem(tp + o, NT)})
        return carry

    lax.fori_loop(1, NT, greet_tp, 0)

    started = []
    used = [0]

    def remote(src, dst, device, sem):
        return pltpu.make_async_remote_copy(
            src_ref=src,
            dst_ref=dst,
            send_sem=send_sem.at[sem],
            recv_sem=recv_sem.at[sem],
            device_id=device,
            device_id_type=MESH,
        )

    def send(src, dst, device, sem):
        copy = remote(src, dst, device, sem)
        copy.start()
        started.append(copy)

    def sems(count):
        first = used[0]
        used[0] += count
        return first

    def wait_bytes(ref, sem):
        pltpu.make_async_copy(ref, ref, sem).wait()

    late = []

    def to_all(axis, src, dst, sem):
        for by in range(1, RING[axis]):
            remote(src(by), dst(by), neighbour(axis, by), sem).start()

    def all_gather(axis, region):
        n = RING[axis]
        order = ring_order(n)
        number = {}
        for step in order:
            for item in step:
                number[item] = len(number)
        first = sems(len(number))
        for j, step in enumerate(order):
            for way, half, k in step:
                by = 1 if way == 0 else -1
                here = hops(n, way, half) - k
                if here > 0:
                    place = region(shifted(axis, -by * here), half)
                    remote(place, place, neighbour(axis, by), first + number[(way, half, k + 1)]).wait_recv()
                place = region(shifted(axis, -by * here), half)
                send(place, place, neighbour(axis, by), first + number[(way, half, k)])
            if j:
                yield j
            else:
                yield 0
            if j + 1 < len(order):
                for way, half, k in step:
                    if k == 1:
                        by = 1 if way == 0 else -1
                        place = region(shifted(axis, -by * (hops(n, way, half))), half)
                        remote(place, place, neighbour(axis, by), first + number[(way, half, 1)]).wait_recv()
        for way, half, k in order[-1]:
            by = 1 if way == 0 else -1
            place = region(shifted(axis, -by * hops(n, way, half)), half)
            remote(place, place, neighbour(axis, by), first + number[(way, half, 1)]).wait_recv()

    def reduce_scatter(axis, own_term, sbuf, rbuf, finish):
        n = RING[axis]
        order = ring_order(n)
        number, slot = {}, {}
        for step in order:
            for item in step:
                number[item] = len(number)
        for way in (0, 1):
            for i, item in enumerate([m for step in order for m in step if m[0] == way]):
                slot[item] = i
        first = sems(len(number))

        def arrival(item):
            way = item[0]
            place = rbuf.at[way, slot[item]]
            remote(sbuf.at[way, slot[item]], place, neighbour(axis, 1 if way == 0 else -1), first + number[item]).wait_recv()

        for j, step in enumerate(order):
            if j == 0:
                for item in step:
                    way, half, k = item
                    value = own_term(shifted(axis, (1 if way == 0 else -1) * k), half)
                    sbuf[way, slot[item]] = value.astype(BF16)
                yield "ready"
            for item in step:
                way, half, k = item
                by = 1 if way == 0 else -1
                if j == 0:
                    send(sbuf.at[way, slot[item]], rbuf.at[way, slot[item]], neighbour(axis, by), first + number[item])
                    continue
                value = own_term(shifted(axis, by * k), half)
                before = (way, half, k + 1)
                arrival(before)
                sbuf[way, slot[item]] = (value + rbuf[way, slot[before]].astype(F32)).astype(BF16)
                send(sbuf.at[way, slot[item]], rbuf.at[way, slot[item]], neighbour(axis, by), first + number[item])
            yield j
        for half in (0, 1):
            value = own_term(pos[axis], half)
            for way in (0, 1):
                arrival((way, half, 1))
                value = value + rbuf[way, slot[(way, half, 1)]].astype(F32)
            finish(half, value)

    def merged(part):
        name, base, rows, axis = part
        r = rows // NX
        prod, sbuf1, rbuf1, share, share16, rbuf2, whole = bufs[name]
        other = "y" if axis == "x" else "x"
        n2 = RING[other]

        for j in range(0, BLOCKS, 2):
            out = dot(wv[base : base + rows], enc[:, j * LANES : (j + 2) * LANES])
            for i in (0, 1):
                prod[j + i] = out[:, i * LANES : (i + 1) * LANES].reshape(NX, r, LANES)

        def term_x(dest, half):
            return prod[half * (NY // 2) : (half + 1) * (NY // 2), dest]

        def term_y(dest, half):
            return prod[dest, half * (NX // 2) : (half + 1) * (NX // 2)]

        def keep(half, value):
            at = pl.ds(half * (n2 // 2), n2 // 2)
            share[at] = value
            share16[at] = value.astype(BF16)

        yield from reduce_scatter(axis, term_x if axis == "x" else term_y, sbuf1, rbuf1, keep)
        sem = sems(2)
        to_all(other, lambda by: share16.at[shifted(other, by)], lambda by: rbuf2.at[by - 1], sem)
        late.append((rbuf2, send_sem.at[sem]))
        yield "scattered"
        total = share[pos[other]]
        wait_bytes(rbuf2, recv_sem.at[sem])
        for i in range(n2 - 1):
            total = total + rbuf2[i].astype(F32)
        whole[y, x] = total.astype(BF16)
        to_all(other, lambda by: whole.at[y, x], lambda by: whole.at[y, x], sem + 1)
        late.append((rbuf2, send_sem.at[sem + 1]))
        yield "shared"
        wait_bytes(rbuf2, recv_sem.at[sem + 1])
        if axis == "x":
            yield from all_gather("x", lambda i, half: whole.at[pl.ds(half * (NY // 2), NY // 2), i])
        else:
            yield from all_gather("y", lambda i, half: whole.at[i, pl.ds(half * (NX // 2), NX // 2)])
        yield "done"

    def attend(row, h, diagonal):
        lanes = slice(h * HEAD, (h + 1) * HEAD)
        keys = kv[0, :, row].reshape(NX * ROWS, HEAD)
        values = kv[1, :, row].reshape(NX * ROWS, HEAD)
        s = nt_dot(qv[:, lanes], keys)
        if diagonal:
            at = lax.broadcasted_iota(jnp.int32, s.shape, 1)
            place = (lax.shift_right_logical(at, 7) & 3) * ROWS + lax.shift_right_logical(at, 9) * 128 + (at & 127)
            mine = x * ROWS + lax.broadcasted_iota(jnp.int32, s.shape, 0)
            s = jnp.where(place <= mine, s, F32(-1e30))
        new_top = jnp.max(s, axis=1, keepdims=True)
        if not diagonal:
            old_top = top[h][:, :1]
            new_top = jnp.maximum(old_top, new_top)
        weights = jnp.exp2((s - new_top) * F32(EXP_SCALE)).astype(BF16)
        extended = jnp.concatenate([values, jnp.ones_like(values)], axis=1)
        update = dot(weights, extended)
        if not diagonal:
            update = update + acc[h] * jnp.exp2((old_top - new_top) * F32(EXP_SCALE))
        acc[h] = update
        top[h] = jnp.broadcast_to(new_top, (ROWS, LANES))

    waiting = []

    def attention():
        for _ in range(NY * HEADS):
            while not waiting:
                step("k")
            row, h, diagonal = waiting.pop(0)
            if diagonal:
                attend(row, h, True)
            else:

                @pl.when(row < y)
                def _():
                    attend(row, h, False)

            yield "attended"
        for h in range(HEADS):
            state = acc[h]
            att[:, h * HEAD : (h + 1) * HEAD] = (state[:, :HEAD] / state[:, HEAD:]).astype(BF16)
        store(att, att_out)

    def keys_and_values():
        gather = all_gather("y", lambda i, half: kv.at[half, core, i, x])

        def spread(row):
            ring = all_gather("x", lambda i, half: kv.at[half, core, row, i])
            next(ring)
            return ring

        def hand_over(row):
            first = sems(2)
            for half in (0, 1):
                place = kv.at[half, core, row]
                send(place, place, {"tp": sibling}, first + half)
            return first

        def handed(row, first):
            for half in (0, 1):
                place = kv.at[half, 1 - core, row]
                remote(place, place, {"tp": sibling}, first + half).wait_recv()

        def arrived(rings):
            for ring in rings:
                for _ in ring:
                    pass

        next(gather)
        before = [spread(y)]
        at = [y]
        yield "sent"
        for k in range(1, NY // 2 + 2):
            rings, rows = [], []
            if k < NY // 2:
                next(gather)
                rows = [shifted("y", -k), shifted("y", k)]
            elif k == NY // 2:
                for _ in gather:
                    pass
                rows = [shifted("y", k)]
            rings = [spread(row) for row in rows]
            for ring in before:
                next(ring)
            yield "sent"
            arrived(before)
            firsts = [hand_over(row) for row in at]
            yield "handed over"
            for row, first in zip(at, firsts):
                handed(row, first)
                waiting.extend((row, h, k == 1) for h in range(HEADS))
            yield "here"
            before, at = rings, rows

    half_tokens = ROWS // 2

    def exchange(group, sem):
        part, from_core, half, recv, full = group

        def z_device(o):
            return {"tp": lax.rem(zi + o, NT // 2) * 2 + core}

        theirs = pl.ds(pl.multiple_of((1 - core) * half_tokens, half_tokens), half_tokens)
        ours = pl.ds(pl.multiple_of(core * half_tokens, half_tokens), half_tokens)

        def to_core():
            return pltpu.make_async_remote_copy(
                src_ref=part.at[theirs],
                dst_ref=from_core,
                send_sem=z_send.at[sem],
                recv_sem=z_recv.at[sem],
                device_id={"tp": sibling},
                device_id_type=MESH,
            )

        to_core().start()
        yield "given"
        to_core().wait_recv()
        half[...] = (part[ours].astype(F32) + from_core[...].astype(F32)).astype(BF16)

        def give(o, carry):
            to = lax.rem(zi + o, NT // 2)
            pltpu.make_async_remote_copy(
                src_ref=half.at[pl.ds(pl.multiple_of(to * SLICE, SLICE), SLICE)],
                dst_ref=recv.at[o - 1],
                send_sem=z_send.at[sem + 1],
                recv_sem=z_recv.at[sem + 1],
                device_id=z_device(o),
                device_id_type=MESH,
            ).start()
            return carry

        lax.fori_loop(1, NT // 2, give, 0)
        yield "scattered"
        total = half[pl.ds(pl.multiple_of(zi * SLICE, SLICE), SLICE)].astype(F32)
        wait_bytes(recv, z_recv.at[sem + 1])
        for o in range(NT // 2 - 1):
            total = total + recv[o].astype(F32)
        mine = pl.ds(pl.multiple_of(core * half_tokens + zi * SLICE, SLICE), SLICE)
        full[mine] = total.astype(BF16)

        def share(o, carry):
            pltpu.make_async_remote_copy(
                src_ref=full.at[mine],
                dst_ref=full.at[mine],
                send_sem=z_send.at[sem + 2],
                recv_sem=z_recv.at[sem + 2],
                device_id=z_device(o),
                device_id_type=MESH,
            ).start()
            return carry

        lax.fori_loop(1, NT // 2, share, 0)
        yield "shared"
        wait_bytes(recv, z_recv.at[sem + 2])

        def whole_half(rows):
            return pltpu.make_async_remote_copy(
                src_ref=full.at[rows],
                dst_ref=full.at[rows],
                send_sem=z_send.at[sem + 3],
                recv_sem=z_recv.at[sem + 3],
                device_id={"tp": sibling},
                device_id_type=MESH,
            )

        whole_half(ours).start()
        yield "handed over"
        whole_half(theirs).wait_recv()
        yield "done"
        to_core().wait_send()
        wait_bytes(recv, z_send.at[sem + 1])
        wait_bytes(recv, z_send.at[sem + 2])
        whole_half(ours).wait_send()

    outs = []

    def store(src, dst):
        copy = pltpu.make_async_copy(src, dst, local_sem.at[len(loads) + len(outs)])
        copy.start()
        outs.append(copy)

    whole = {name: bufs[name][6] for name, *_ in PARTS}
    rows_of = {name: rows for name, _, rows, _ in PARTS}

    def block(name, j):
        return whole[name][j].reshape(rows_of[name], LANES)

    def code(g):
        for name in "uac":
            finish(name)
        reach("b", READY[g])
        for i, by in enumerate(GROUPS[g]):
            j = shifted("y", by)
            total = dot(hid[:, :SPLIT], block("a", j)) + dot(hid[:, SPLIT:], block("b", j)) + dot(att[...], block("c", j))
            code_refs[g][0][:, i * LANES : (i + 1) * LANES] = total.astype(BF16)
        yield from exchange(code_refs[g], 4 + 4 * g)

    def back(name):
        total = None
        for j in range(0, BLOCKS, 2):
            pair = jnp.concatenate([block(name, j), block(name, j + 1)], axis=1)
            term = nt_dot(grad_refs[4][:, LANES * j : LANES * (j + 2)], pair)
            total = term if total is None else total + term
        return total.astype(BF16)

    def gradients():
        finish("g")
        finish("a")
        gh[:, :SPLIT] = back("a")
        yield "first"
        finish("b")
        gh[:, SPLIT:] = back("b")
        store(gh, gh_out)
        yield "second"
        finish("c")
        ga[...] = back("c")
        store(ga, ga_out)
        yield "third"

    gens = {part[0]: merged(part) for part in PARTS}
    gens.update(k=keys_and_values(), u=attention(), g=exchange(grad_refs, 0), m=gradients())
    gens.update({str(g): code(g) for g in range(len(GROUPS))})
    taken = {name: 0 for name in gens}
    ended = set()

    def step(name):
        taken[name] += 1
        if name not in ended and next(gens[name], None) is None:
            ended.add(name)

    def finish(name):
        while name not in ended:
            step(name)

    def reach(name, count):
        while taken[name] < count and name not in ended:
            step(name)

    for name in ("dw", "ow", "enc"):
        loads[name].wait()
    for name in "acb":
        step(name)
    loads["cot"].wait()
    loads["dec"].wait()
    grad_refs[0][...] = nt_dot(cot[...], dec[...]).astype(BF16)
    for name in ("k", "v", "q", "hid"):
        loads[name].wait()
    pl.semaphore_wait(barrier, NX - 1 + NY - 1 + NT - 1)
    for name in "".join(ORDER):
        step(name)
    result = None
    for g, cols in enumerate(GROUPS):
        reach(str(g), 5)
        for i, by in enumerate(cols):
            rows = pl.ds(pl.multiple_of(shifted("y", by) * LANES, LANES), LANES)
            term = dot(code_refs[g][4][:, i * LANES : (i + 1) * LANES], dec[rows])
            result = term if result is None else result + term
    decd[...] = result.astype(BF16)
    store(decd, dec_out)
    for name in gens:
        finish(name)
    for copy in started:
        copy.wait_send()
    for ref, sem in late:
        wait_bytes(ref, sem)
    for copy in outs:
        copy.wait()


def deliver(*refs):
    ins, outs, held, sems = refs[:4], refs[4:8], refs[8:12], refs[12]
    loads = [pltpu.make_async_copy(ins[i], held[i], sems.at[i]) for i in range(4)]
    stores = [pltpu.make_async_copy(held[i], outs[i], sems.at[4 + i]) for i in range(4)]
    for copy in loads:
        copy.start()
    for copy, then in zip(loads, stores):
        copy.wait()
        then.start()
    for copy in stores:
        copy.wait()


def per_device(*args):
    anywhere = pl.BlockSpec(memory_space=pl.ANY)
    scratch = [
        pltpu.VMEM((ROWS, ATT_HERE), BF16),
        pltpu.VMEM((ROWS, FF_HERE), BF16),
        pltpu.VMEM((FF_HERE + ATT_HERE, 256), BF16),
        pltpu.VMEM((256, R), BF16),
        pltpu.VMEM((R, 512), BF16),
        pltpu.VMEM((ROWS, 512), BF16),
        pltpu.VMEM((2, 2, NY, NX, 128, HEAD), BF16),
        pltpu.VMEM((HEADS, ROWS, 2 * HEAD), F32),
        pltpu.VMEM((HEADS, ROWS, LANES), F32),
        pltpu.VMEM((ROWS, ATT_HERE), BF16),
        pltpu.VMEM((ROWS, 512), BF16),
        pltpu.VMEM((ROWS, FF_HERE), BF16),
        pltpu.VMEM((ROWS, ATT_HERE), BF16),
    ]
    for width in (R, *(LANES * len(cols) for cols in GROUPS)):
        scratch += [
            pltpu.VMEM((ROWS, width), BF16),
            pltpu.VMEM((ROWS // 2, width), BF16),
            pltpu.VMEM((ROWS // 2, width), BF16),
            pltpu.VMEM((NT // 2 - 1, SLICE, width), BF16),
            pltpu.VMEM((ROWS, width), BF16),
        ]
    for part in PARTS:
        scratch += scratch_of(part)
    scratch += [
        pltpu.SemaphoreType.DMA((SEMS,)),
        pltpu.SemaphoreType.DMA((SEMS,)),
        pltpu.SemaphoreType.DMA((4 + 4 * len(GROUPS),)),
        pltpu.SemaphoreType.DMA((4 + 4 * len(GROUPS),)),
        pltpu.SemaphoreType.DMA((LOCAL,)),
    ]
    shapes = (
        jax.ShapeDtypeStruct((ROWS, ATT_HERE), BF16),
        jax.ShapeDtypeStruct((ROWS, 512), BF16),
        jax.ShapeDtypeStruct((ROWS, FF_HERE), BF16),
        jax.ShapeDtypeStruct((ROWS, ATT_HERE), BF16),
    )
    results = pl.pallas_call(
        kernel,
        out_shape=shapes,
        in_specs=[anywhere] * 9,
        out_specs=(anywhere,) * 4,
        scratch_shapes=scratch,
        compiler_params=pltpu.CompilerParams(
            collective_id=0, has_side_effects=True, vmem_limit_bytes=56 * 1024 * 1024
        ),
    )(*args)
    return pl.pallas_call(
        deliver,
        out_shape=shapes,
        in_specs=[anywhere] * 4,
        out_specs=(anywhere,) * 4,
        scratch_shapes=[pltpu.VMEM(shape.shape, BF16) for shape in shapes] + [pltpu.SemaphoreType.DMA((8,))],
        compiler_params=pltpu.CompilerParams(vmem_limit_bytes=60 * 1024 * 1024),
    )(*results)


def solution(mesh):
    return jax.shard_map(
        per_device,
        mesh=mesh,
        in_specs=(
            P("ctx", "tp"),
            P("ctx", None),
            P("ctx", None),
            P("ctx", "tp"),
            P("tp", "ctx"),
            P("tp", "ctx"),
            P("ctx", None),
            P(None, "tp"),
            P("ctx", "tp"),
        ),
        out_specs=(P("ctx", "tp"), P("ctx", "tp"), P("ctx", "tp"), P("ctx", "tp")),
        check_vma=False,
    )
```

time: 141 us -> 97.4 us (0.69)
  Pallas kernels: 136 us -> 96.4 us
  local copies, waits for them, and re-layouts: 4.24 us -> 0 us
    pallas_call x1 -> x2, Pallas kernels: 136 us -> 96.4 us  [the longest x1 94.3 us: per_device(): pl.pallas_call(kernel, out_shape=shapes, in_specs=[anywhere] * 9, out_spe...]
    unnamed x10 -> x0, local copies, waits for them, and re-layouts: 4.24 us -> none
where the time goes in v2:
time: 97.4 us; the launch traced here: 97.2 us
  Pallas kernels  96.4 us (99%)
    pallas_call x1, Pallas kernels, per_device(): pl.pallas_call(kernel, out_shape=shapes, in_specs=[anywhere] * 9, out_spe...  94.3 us
    pallas_call x1, Pallas kernels, per_device(): pl.pallas_call(deliver, out_shape=shapes, in_specs=[anywhere] * 4, out_sp...  2.1 us

profile of v2, /device:TPU:1, one launch (start us, length us, event | category | flops | bytes accessed | tf_op | source)
XLA Modules:
  0.0 97.2 jit_solution(14871900970611337155)
XLA Ops:
  0.6 94.3 %shard_map.120 = (bf16[256,512]{1,0:T(8,128)(2,1)}, bf16[256,512]{1,0:T(8,128)(2,1)}, bf16[256,896]{1,0:T(8,128)(2,1)}, bf16[256,512]{1,0:T(8,128)(2,1)}) custom-call(bf16[256,512]{1,0:T(8,128)(2,1)} %refs_0_.1, bf16[256,1024]{1,0:T(8,128)(2,1)} %refs_1_.1, bf16[256,1024]{1,0:T(8,128)(2,1)} %refs_2_.1, bf16[256,896]{1,0:T(8,128)(2,1)} %refs_3_.1, ...), custom_call_target="tpu_custom_call" | custom-call | tf_op jit(solution)/shard_map/pallas_call | solution.py:626
  94.9 2.1 %shard_map.121 = (bf16[256,512]{1,0:T(8,128)(2,1)}, bf16[256,512]{1,0:T(8,128)(2,1)}, bf16[256,896]{1,0:T(8,128)(2,1)}, bf16[256,512]{1,0:T(8,128)(2,1)}) custom-call(bf16[256,512]{1,0:T(8,128)(2,1)} %get-tuple-element.8.refs_0_, bf16[256,512]{1,0:T(8,128)(2,1)} %get-tuple-element.9.refs_1_, bf16[256,896]{1,0:T(8,128)(2,1)} %get-tuple-element.10.refs_2_, ...), custom_call_target="tpu_custom_call" | custom-call | tf_op jit(solution)/shard_map/pallas_call | solution.py:636

commit v3 on v2

--- a/solution.py
+++ b/solution.py
@@ -20,11 +20,11 @@
 FF_HERE, ATT_HERE = 896, 512
 SLICE = ROWS // NT
 ORDER = (
-    "kagkcbabkgacukabcuaukgubkkuuubcaukuuubuuaukubuuuca",
-    "kubuukauuuubcukua02cu013cbck31g20kau3ck12mbuucmccm",
-    "bckcgckga3uu",
+    "kagkcabkgacubuakbuackgbauukuuauubckuuuabkukuuubguu",
+    "uckuabuukuuuauckb02013uk1m2ckc0ukb3kc12cckmmcac3cb",
+    "uuubacggcuu",
 )
-READY = (9, 10, 11, 12)
+READY = (8, 9, 10, 11)
 GROUPS = ((0, 1, -1), (2, -2), (3, -3), (4,))
 EXP_SCALE = math.log2(math.e) / math.sqrt(HEAD)
 PARTS = (("a", 0, 512, "y"), ("b", 512, 384, "y"), ("c", 896, 512, "x"))
@@ -55,6 +55,10 @@
                     step.append((way, half, k))
         steps.append(step)
     return steps
+
+
+def farthest_first(n):
+    return range(1, n)
 
 
 def copies_of_ring(n):
@@ -95,7 +99,7 @@
     qv, hid, wv, enc, dec, cot, kv = take(7)
     acc, top, att, decd, gh, ga = take(6)
     grad_refs = take(5)
-    code_refs = [take(5) for _ in GROUPS]
+    code_refs = [take(5) for _ in GROUPS[1:]] + [take(3)]
     bufs = {part[0]: take(7) for part in PARTS}
     send_sem, recv_sem, z_send, z_recv, local_sem = take(5)
     assert not rest
@@ -135,6 +139,14 @@
     load("q", q_in, qv)
     load("hid", hid_in, hid)
 
+    awaited = set()
+
+    def loaded(*names):
+        for name in names:
+            if name not in awaited:
+                awaited.add(name)
+                loads[name].wait()
+
     barrier = pltpu.get_barrier_semaphore()
 
     def greet(device):
@@ -179,7 +191,7 @@
     late = []
 
     def to_all(axis, src, dst, sem):
-        for by in range(1, RING[axis]):
+        for by in farthest_first(RING[axis]):
             remote(src(by), dst(by), neighbour(axis, by), sem).start()
 
     def all_gather(axis, region):
@@ -237,7 +249,6 @@
                     way, half, k = item
                     value = own_term(shifted(axis, (1 if way == 0 else -1) * k), half)
                     sbuf[way, slot[item]] = value.astype(BF16)
-                yield "ready"
             for item in step:
                 way, half, k = item
                 by = 1 if way == 0 else -1
@@ -264,6 +275,7 @@
         other = "y" if axis == "x" else "x"
         n2 = RING[other]
 
+        loaded("dw" if base < FF_HERE else "ow", "enc")
         for j in range(0, BLOCKS, 2):
             out = dot(wv[base : base + rows], enc[:, j * LANES : (j + 2) * LANES])
             for i in (0, 1):
@@ -325,6 +337,7 @@
     waiting = []
 
     def attention():
+        loaded("q")
         for _ in range(NY * HEADS):
             while not waiting:
                 step("k")
@@ -344,6 +357,7 @@
         store(att, att_out)
 
     def keys_and_values():
+        loaded("k", "v")
         gather = all_gather("y", lambda i, half: kv.at[half, core, i, x])
 
         def spread(row):
@@ -420,7 +434,7 @@
         to_core().wait_recv()
         half[...] = (part[ours].astype(F32) + from_core[...].astype(F32)).astype(BF16)
 
-        def give(o, carry):
+        def give(o):
             to = lax.rem(zi + o, NT // 2)
             pltpu.make_async_remote_copy(
                 src_ref=half.at[pl.ds(pl.multiple_of(to * SLICE, SLICE), SLICE)],
@@ -430,9 +444,9 @@
                 device_id=z_device(o),
                 device_id_type=MESH,
             ).start()
-            return carry
-
-        lax.fori_loop(1, NT // 2, give, 0)
+
+        for o in farthest_first(NT // 2):
+            give(o)
         yield "scattered"
         total = half[pl.ds(pl.multiple_of(zi * SLICE, SLICE), SLICE)].astype(F32)
         wait_bytes(recv, z_recv.at[sem + 1])
@@ -441,7 +455,7 @@
         mine = pl.ds(pl.multiple_of(core * half_tokens + zi * SLICE, SLICE), SLICE)
         full[mine] = total.astype(BF16)
 
-        def share(o, carry):
+        def share(o):
             pltpu.make_async_remote_copy(
                 src_ref=full.at[mine],
                 dst_ref=full.at[mine],
@@ -450,9 +464,9 @@
                 device_id=z_device(o),
                 device_id_type=MESH,
             ).start()
-            return carry
-
-        lax.fori_loop(1, NT // 2, share, 0)
+
+        for o in farthest_first(NT // 2):
+            share(o)
         yield "shared"
         wait_bytes(recv, z_recv.at[sem + 2])
 
@@ -475,6 +489,42 @@
         wait_bytes(recv, z_send.at[sem + 2])
         whole_half(ours).wait_send()
 
+    def exchange_straight(group, sem):
+        part, recv, full = group
+        mine = pl.ds(pl.multiple_of(tp * SLICE, SLICE), SLICE)
+
+        def to_each(src, dst, at):
+            for apart in farthest_first(NT // 2):
+                for other in (0, 1):
+                    one(apart, other, src, dst, at)
+            one(0, 1, src, dst, at)
+
+        def one(apart, other, src, dst, at):
+            z = lax.rem(zi + apart, NT // 2)
+            to = z * 2 + (core if other == 0 else 1 - core)
+            pltpu.make_async_remote_copy(
+                src_ref=src(to),
+                dst_ref=dst(2 * apart + other - 1),
+                send_sem=z_send.at[sem + at],
+                recv_sem=z_recv.at[sem + at],
+                device_id={"tp": to},
+                device_id_type=MESH,
+            ).start()
+
+        to_each(lambda to: part.at[pl.ds(pl.multiple_of(to * SLICE, SLICE), SLICE)], lambda slot: recv.at[slot], 0)
+        yield "scattered"
+        total = part[mine].astype(F32)
+        wait_bytes(recv, z_recv.at[sem])
+        for o in range(NT - 1):
+            total = total + recv[o].astype(F32)
+        full[mine] = total.astype(BF16)
+        to_each(lambda to: full.at[mine], lambda slot: full.at[mine], 1)
+        yield "shared"
+        wait_bytes(recv, z_recv.at[sem + 1])
+        yield "done"
+        for at in (0, 1):
+            wait_bytes(recv, z_send.at[sem + at])
+
     outs = []
 
     def store(src, dst):
@@ -488,7 +538,13 @@
     def block(name, j):
         return whole[name][j].reshape(rows_of[name], LANES)
 
+    def grad_code():
+        loaded("cot", "dec")
+        grad_refs[0][...] = nt_dot(cot[...], dec[...]).astype(BF16)
+        yield from exchange(grad_refs, 0)
+
     def code(g):
+        loaded("hid")
         for name in "uac":
             finish(name)
         reach("b", READY[g])
@@ -496,7 +552,10 @@
             j = shifted("y", by)
             total = dot(hid[:, :SPLIT], block("a", j)) + dot(hid[:, SPLIT:], block("b", j)) + dot(att[...], block("c", j))
             code_refs[g][0][:, i * LANES : (i + 1) * LANES] = total.astype(BF16)
-        yield from exchange(code_refs[g], 4 + 4 * g)
+        if g == len(GROUPS) - 1:
+            yield from exchange_straight(code_refs[g], 4 + 4 * g)
+        else:
+            yield from exchange(code_refs[g], 4 + 4 * g)
 
     def back(name):
         total = None
@@ -521,15 +580,25 @@
         yield "third"
 
     gens = {part[0]: merged(part) for part in PARTS}
-    gens.update(k=keys_and_values(), u=attention(), g=exchange(grad_refs, 0), m=gradients())
+    gens.update(k=keys_and_values(), u=attention(), g=grad_code(), m=gradients())
     gens.update({str(g): code(g) for g in range(len(GROUPS))})
     taken = {name: 0 for name in gens}
     ended = set()
+
+    def sent():
+        for copy in started:
+            copy.wait_send()
+        started.clear()
+        for ref, sem in late:
+            wait_bytes(ref, sem)
+        late.clear()
 
     def step(name):
         taken[name] += 1
         if name not in ended and next(gens[name], None) is None:
             ended.add(name)
+        if name == str(len(GROUPS) - 1) and taken[name] == 2:
+            sent()
 
     def finish(name):
         while name not in ended:
@@ -539,15 +608,6 @@
         while taken[name] < count and name not in ended:
             step(name)
 
-    for name in ("dw", "ow", "enc"):
-        loads[name].wait()
-    for name in "acb":
-        step(name)
-    loads["cot"].wait()
-    loads["dec"].wait()
-    grad_refs[0][...] = nt_dot(cot[...], dec[...]).astype(BF16)
-    for name in ("k", "v", "q", "hid"):
-        loads[name].wait()
     pl.semaphore_wait(barrier, NX - 1 + NY - 1 + NT - 1)
     for name in "".join(ORDER):
         step(name)
@@ -556,16 +616,13 @@
         reach(str(g), 5)
         for i, by in enumerate(cols):
             rows = pl.ds(pl.multiple_of(shifted("y", by) * LANES, LANES), LANES)
-            term = dot(code_refs[g][4][:, i * LANES : (i + 1) * LANES], dec[rows])
+            term = dot(code_refs[g][-1][:, i * LANES : (i + 1) * LANES], dec[rows])
             result = term if result is None else result + term
     decd[...] = result.astype(BF16)
     store(decd, dec_out)
     for name in gens:
         finish(name)
-    for copy in started:
-        copy.wait_send()
-    for ref, sem in late:
-        wait_bytes(ref, sem)
+    sent()
     for copy in outs:
         copy.wait()
 
@@ -600,7 +657,7 @@
         pltpu.VMEM((ROWS, FF_HERE), BF16),
         pltpu.VMEM((ROWS, ATT_HERE), BF16),
     ]
-    for width in (R, *(LANES * len(cols) for cols in GROUPS)):
+    for width in (R, *(LANES * len(cols) for cols in GROUPS[:-1])):
         scratch += [
             pltpu.VMEM((ROWS, width), BF16),
             pltpu.VMEM((ROWS // 2, width), BF16),
@@ -608,6 +665,8 @@
             pltpu.VMEM((NT // 2 - 1, SLICE, width), BF16),
             pltpu.VMEM((ROWS, width), BF16),
         ]
+    width = LANES * len(GROUPS[-1])
+    scratch += [pltpu.VMEM((ROWS, width), BF16), pltpu.VMEM((NT - 1, SLICE, width), BF16), pltpu.VMEM((ROWS, width), BF16)]
     for part in PARTS:
         scratch += scratch_of(part)
     scratch += [

time: 97.4 us -> 96.3 us (0.989)
  Pallas kernels: 96.4 us -> 95.3 us
    pallas_call x1, Pallas kernels: 94.3 us -> 93.2 us  [per_device(): pl.pallas_call(kernel, out_shape=shapes, in_specs=[anywhere] * 9, out_spe...]
where the time goes in v3:
time: 96.3 us; the launch traced here: 96.2 us
  Pallas kernels  95.3 us (99%)
    pallas_call x1, Pallas kernels, per_device(): pl.pallas_call(kernel, out_shape=shapes, in_specs=[anywhere] * 9, out_spe...  93.2 us
    pallas_call x1, Pallas kernels, per_device(): pl.pallas_call(deliver, out_shape=shapes, in_specs=[anywhere] * 4, out_sp...  2.1 us

profile of v3, /device:TPU:1, one launch (start us, length us, event | category | flops | bytes accessed | tf_op | source)
XLA Modules:
  0.0 96.2 jit_solution(1069042186882145714)
XLA Ops:
  0.6 93.2 %shard_map.120 = (bf16[256,512]{1,0:T(8,128)(2,1)}, bf16[256,512]{1,0:T(8,128)(2,1)}, bf16[256,896]{1,0:T(8,128)(2,1)}, bf16[256,512]{1,0:T(8,128)(2,1)}) custom-call(bf16[256,512]{1,0:T(8,128)(2,1)} %refs_0_.1, bf16[256,1024]{1,0:T(8,128)(2,1)} %refs_1_.1, bf16[256,1024]{1,0:T(8,128)(2,1)} %refs_2_.1, bf16[256,896]{1,0:T(8,128)(2,1)} %refs_3_.1, ...), custom_call_target="tpu_custom_call" | custom-call | tf_op jit(solution)/shard_map/pallas_call | solution.py:685
  93.9 2.1 %shard_map.121 = (bf16[256,512]{1,0:T(8,128)(2,1)}, bf16[256,512]{1,0:T(8,128)(2,1)}, bf16[256,896]{1,0:T(8,128)(2,1)}, bf16[256,512]{1,0:T(8,128)(2,1)}) custom-call(bf16[256,512]{1,0:T(8,128)(2,1)} %get-tuple-element.8.refs_0_, bf16[256,512]{1,0:T(8,128)(2,1)} %get-tuple-element.9.refs_1_, bf16[256,896]{1,0:T(8,128)(2,1)} %get-tuple-element.10.refs_2_, ...), custom_call_target="tpu_custom_call" | custom-call | tf_op jit(solution)/shard_map/pallas_call | solution.py:695
